TPU v7x, 128 devices: a whole 4x4x4 slice. The times are simulated.
128 devices in a mesh: day: 4 (over x), chan: 32 (over y, z, core).
Axes of the slice: x: 4, y: 4, z: 4, core: 2. Of those that a mesh axis runs over, the one named last changes fastest.
Arguments:
- strain_raw: bfloat16 [8, 4096, 1024], P('day', 'chan'), may hold values from -320 to 320, as said below
- pair_dist: int32 [32, 3], P('chan'), may hold values from -1 to 4, as said below
Outputs:
- stack: float32 [96, 129, 128, 128], P('chan', None, 'day')
Inputs may be any that keep to these rules, and one draw needn't show every extreme that they name: `pair_dist`: each owner's live slots come first and hold distinct distances with c + distance below 32; every owner has at least one live slot and owner 0 has all 3 live, one of them at distance 4. `strain_raw`: channels differ in scale and offset.
All inputs are finite; a program needn't handle non-finite values.
Results may differ from a plain program's by a relative error of at most 0.0039.
Values may be sent and summed in bfloat16 or wider, within the bound.
No kernel may reach another device: no remote copies, remote signals or barrier semaphores. Data moves between devices by JAX's collectives and lax.ppermute only.
A program may use at most 256 MiB of HBM per device.

v0:
```python
import jax
import jax.numpy as jnp
from jax import lax
from jax.sharding import PartitionSpec as P

BW = 128
SAMPLES = 1024
MAXLAG = 64
REACH = 4
TILES_DEV = 3


lag_group = 32


def passed_along(array, axis, by):
    devices = lax.axis_size(axis)
    pairs = [(i, i + by) for i in range(devices) if 0 <= i + by < devices]
    return lax.ppermute(array, axis, pairs)


def whiten_local(strain_raw):
    values = strain_raw.astype(jnp.float32)
    centred = values - jnp.mean(values, axis=-1, keepdims=True)
    spread = jnp.mean(centred * centred, axis=-1, keepdims=True)
    return (centred * lax.rsqrt(spread + 1e-06)).astype(jnp.bfloat16)


def fetch_blocks(local_days):
    pieces = [local_days] + [
        passed_along(local_days, "chan", -step) for step in range(1, REACH + 1)
    ]
    return jnp.stack(pieces, 0)


def correlate(left_rows, partner, lag_count):
    left_pad = jnp.pad(left_rows, ((0, 0), (0, 0), (MAXLAG, MAXLAG)))
    results = []
    for first_lag in range(0, lag_count, lag_group):
        last_lag = min(first_lag + lag_group, lag_count)
        shifted = jnp.stack(
            [
                left_pad[:, :, 2 * MAXLAG - lag : 2 * MAXLAG - lag + SAMPLES]
                for lag in range(first_lag, last_lag)
            ],
            0,
        )
        results.append(
            jnp.einsum("ldis,djs->lij", shifted, partner, preferred_element_type=jnp.float32)
        )
    return jnp.concatenate(results, 0)


def local(strain_raw, pair_dist):
    whitened = whiten_local(strain_raw)
    day_count = lax.axis_size("day")
    total_days = whitened.shape[0] * day_count
    lag_count = 2 * MAXLAG + 1
    local_days = lax.all_gather(whitened, "day", axis=0, tiled=True)
    row_count = BW // day_count
    left_rows = lax.dynamic_slice_in_dim(
        local_days, lax.axis_index("day") * row_count, row_count, 1
    )
    candidates = fetch_blocks(local_days)
    norm = 1.0 / jnp.sqrt(jnp.float32(SAMPLES * total_days))
    tiles = []
    for slot in range(TILES_DEV):
        distance = pair_dist[0, slot]
        partner = lax.dynamic_index_in_dim(candidates, jnp.maximum(distance, 0), 0, keepdims=False)
        tile = correlate(left_rows, partner, lag_count) * norm
        tiles.append(jnp.where(distance >= 0, tile, jnp.zeros_like(tile)))
    partial_tiles = jnp.stack(tiles, 0)
    return partial_tiles


def solution(mesh):
    placed = (P("day", "chan", None), P("chan", None))
    return jax.shard_map(
        local, mesh=mesh, in_specs=placed, out_specs=P("chan", None, "day", None), check_vma=False
    )
```

profile of v0, /device:TPU:64, one launch (start us, length us, event | category | flops | bytes accessed | tf_op | source)
XLA Modules:
  0.0 440.2 jit_solution(4861122382386660306)
XLA Ops:
  6.5 1.2 convert_reduce_fusion
  7.7 1.3 fusion.137
  9.1 2.1 fusion.138
  11.2 1.4 fusion.160
  16.0 27.8 %all-gather.2.cloned.1.call-done = bf16[8,128,1024]{2,1,0:T(8,128)(2,1)} async-done(((bf16[2,128,1024]{2,1,0:T(8,128)(2,1)}), bf16[8,128,1024]{2,1,0:T(8,128)(2,1)}) %all-gather.2.cloned.1.call-update) | async-done | bytes 2097168 | tf_op jit(solution)/shard_map/all_gather | solution.py:59
  43.8 1.1 bitcast_dynamic-update-slice_fusion.68
  51.8 1.2 bitcast_dynamic-update-slice_fusion.7
  53.0 1.2 bitcast_dynamic-update-slice_fusion.6
  54.2 1.2 bitcast_dynamic-update-slice_fusion.130
  55.4 1.6 bitcast_dynamic-update-slice_fusion.129
  57.1 3.2 copy-done.3
  60.2 1.6 bitcast_dynamic-update-slice_fusion.5
  69.0 1.3 bitcast_dynamic-update-slice_fusion.37
  72.1 3.9 copy-done.2
  80.8 1.3 bitcast_dynamic-update-slice_fusion.69
  82.1 1.2 bitcast_dynamic-update-slice_fusion.125
  83.3 1.6 bitcast_dynamic-update-slice_fusion.124
  84.9 1.9 bitcast_dynamic-update-slice_fusion.123
  86.8 1.7 bitcast_dynamic-update-slice_fusion.122
  88.5 1.4 bitcast_dynamic-update-slice_fusion.121
  89.9 1.1 bitcast_dynamic-update-slice_fusion.120
  95.1 1.9 collective-permute-start
  98.0 2.4 collective-permute-start.1
  100.4 1.1 bitcast_dynamic-update-slice_fusion.114
  101.5 1.1 bitcast_dynamic-update-slice_fusion.113
  103.5 1.9 collective-permute-start.2
  105.5 1.9 collective-permute-start.3
  108.4 1.0 bitcast_dynamic-update-slice_fusion.110
  112.5 1.0 bitcast_dynamic-update-slice_fusion.106
  116.6 1.1 bitcast_dynamic-update-slice_fusion.102
  117.7 1.0 bitcast_dynamic-update-slice_fusion.101
  118.9 21.1 %collective-permute-done = bf16[8,128,1024]{2,1,0:T(8,128)(2,1)S(1)} collective-permute-done((bf16[8,128,1024]{2,1,0:T(8,128)(2,1)S(1)}, bf16[8,128,1024]{2,1,0:T(8,128)(2,1)S(1)}, u32[]{:S(2)}, u32[]{:S(2)}) %collective-permute-start) | collective-permute-done | bytes 2097184 | tf_op jit(solution)/shard_map/ppermute | solution.py:19
  140.2 46.5 %collective-permute-done.1 = bf16[8,128,1024]{2,1,0:T(8,128)(2,1)S(1)} collective-permute-done((bf16[8,128,1024]{2,1,0:T(8,128)(2,1)S(1)}, bf16[8,128,1024]{2,1,0:T(8,128)(2,1)S(1)}, u32[]{:S(2)}, u32[]{:S(2)}) %collective-permute-start.1) | collective-permute-done | bytes 2097184 | tf_op jit(solution)/shard_map/ppermute | solution.py:19
  187.0 6.0 %collective-permute-done.2 = bf16[8,128,1024]{2,1,0:T(8,128)(2,1)S(1)} collective-permute-done((bf16[8,128,1024]{2,1,0:T(8,128)(2,1)S(1)}, bf16[8,128,1024]{2,1,0:T(8,128)(2,1)S(1)}, u32[]{:S(2)}, u32[]{:S(2)}) %collective-permute-start.2) | collective-permute-done | bytes 2097184 | tf_op jit(solution)/shard_map/ppermute | solution.py:19
  193.2 133.6 %collective-permute-done.3 = bf16[8,128,1024]{2,1,0:T(8,128)(2,1)S(1)} collective-permute-done((bf16[8,128,1024]{2,1,0:T(8,128)(2,1)S(1)}, bf16[8,128,1024]{2,1,0:T(8,128)(2,1)S(1)}, u32[]{:S(2)}, u32[]{:S(2)}) %collective-permute-start.3) | collective-permute-done | bytes 2097184 | tf_op jit(solution)/shard_map/ppermute | solution.py:19
  327.1 8.4 %fusion.35 = f32[1,129,32,128]{3,2,1,0:T(8,128)S(1)} fusion(bf16[32,8,32,1024]{3,2,1,0:T(8,128)(2,1)} %bitcast_dynamic-update-slice_fusion.101, bf16[5,8,128,1024]{3,2,1,0:T(8,128)(2,1)S(1)} %bitcast_dynamic-update-slice_fusion, s32[]{:T(128)} %bitcast.38), kind=kOutput, calls=%fused_computation.44 | convolution fusion | flops 2147483648 | bytes 19398660 | tf_op jit(solution)/shard_map/ldis,djs->lij/dot_general | solution.py:49
  335.4 8.2 %fusion.41 = f32[1,129,32,128]{3,2,1,0:T(8,128)S(1)} fusion(f32[1,129,32,128]{3,2,1,0:T(8,128)S(1)} %fusion.35, bf16[32,8,32,1024]{3,2,1,0:T(8,128)(2,1)} %copy-done.1, bf16[5,8,128,1024]{3,2,1,0:T(8,128)(2,1)S(1)} %bitcast_dynamic-update-slice_fusion, s32[]{:T(128)} %bitcast.38), kind=kOutput, calls=%fused_computation.46 | convolution fusion | flops 2147483648 | bytes 19398660 | tf_op jit(solution)/shard_map/ldis,djs->lij/dot_general | solution.py:49
  343.6 8.2 %fusion.47 = f32[1,129,32,128]{3,2,1,0:T(8,128)S(1)} fusion(f32[1,129,32,128]{3,2,1,0:T(8,128)S(1)} %fusion.41, bf16[32,8,32,1024]{3,2,1,0:T(8,128)(2,1)} %copy-done.2, bf16[5,8,128,1024]{3,2,1,0:T(8,128)(2,1)S(1)} %bitcast_dynamic-update-slice_fusion, s32[]{:T(128)} %bitcast.38), kind=kOutput, calls=%fused_computation.48 | convolution fusion | flops 2147483648 | bytes 19398660 | tf_op jit(solution)/shard_map/ldis,djs->lij/dot_general | solution.py:49
  351.8 8.2 %fusion.53 = f32[1,129,32,128]{3,2,1,0:T(8,128)S(1)} fusion(f32[1,129,32,128]{3,2,1,0:T(8,128)S(1)} %fusion.47, bf16[32,8,32,1024]{3,2,1,0:T(8,128)(2,1)} %get-tuple-element.7, bf16[5,8,128,1024]{3,2,1,0:T(8,128)(2,1)S(1)} %bitcast_dynamic-update-slice_fusion, s32[]{:T(128)} %bitcast.38), kind=kOutput, calls=%fused_computation.50 | convolution fusion | flops 2147483648 | bytes 19398660 | tf_op jit(solution)/shard_map/ldis,djs->lij/dot_general | solution.py:49
  360.9 8.2 %fusion.59 = f32[1,129,32,128]{3,2,1,0:T(8,128)S(1)} fusion(bf16[32,8,32,1024]{3,2,1,0:T(8,128)(2,1)} %bitcast_dynamic-update-slice_fusion.101, bf16[5,8,128,1024]{3,2,1,0:T(8,128)(2,1)S(1)} %bitcast_dynamic-update-slice_fusion, s32[]{:T(128)} %bitcast.152), kind=kOutput, calls=%fused_computation.52 | convolution fusion | flops 2147483648 | bytes 19398660 | tf_op jit(solution)/shard_map/ldis,djs->lij/dot_general | solution.py:49
  369.1 8.4 %fusion.65 = f32[1,129,32,128]{3,2,1,0:T(8,128)S(1)} fusion(f32[1,129,32,128]{3,2,1,0:T(8,128)S(1)} %fusion.59, bf16[32,8,32,1024]{3,2,1,0:T(8,128)(2,1)} %copy-done.1, bf16[5,8,128,1024]{3,2,1,0:T(8,128)(2,1)S(1)} %bitcast_dynamic-update-slice_fusion, s32[]{:T(128)} %bitcast.152), kind=kOutput, calls=%fused_computation.54 | convolution fusion | flops 2147483648 | bytes 19398660 | tf_op jit(solution)/shard_map/ldis,djs->lij/dot_general | solution.py:49
  377.5 8.2 %fusion.71 = f32[1,129,32,128]{3,2,1,0:T(8,128)S(1)} fusion(f32[1,129,32,128]{3,2,1,0:T(8,128)S(1)} %fusion.65, bf16[32,8,32,1024]{3,2,1,0:T(8,128)(2,1)} %copy-done.2, bf16[5,8,128,1024]{3,2,1,0:T(8,128)(2,1)S(1)} %bitcast_dynamic-update-slice_fusion, s32[]{:T(128)} %bitcast.152), kind=kOutput, calls=%fused_computation.56 | convolution fusion | flops 2147483648 | bytes 19398660 | tf_op jit(solution)/shard_map/ldis,djs->lij/dot_general | solution.py:49
  385.7 8.2 %fusion.77 = f32[1,129,32,128]{3,2,1,0:T(8,128)S(1)} fusion(f32[1,129,32,128]{3,2,1,0:T(8,128)S(1)} %fusion.71, bf16[32,8,32,1024]{3,2,1,0:T(8,128)(2,1)} %get-tuple-element.7, bf16[5,8,128,1024]{3,2,1,0:T(8,128)(2,1)S(1)} %bitcast_dynamic-update-slice_fusion, s32[]{:T(128)} %bitcast.152), kind=kOutput, calls=%fused_computation.58 | convolution fusion | flops 2147483648 | bytes 19398660 | tf_op jit(solution)/shard_map/ldis,djs->lij/dot_general | solution.py:49
  394.7 8.2 %fusion.83 = f32[1,129,32,128]{3,2,1,0:T(8,128)S(1)} fusion(bf16[32,8,32,1024]{3,2,1,0:T(8,128)(2,1)} %bitcast_dynamic-update-slice_fusion.101, bf16[5,8,128,1024]{3,2,1,0:T(8,128)(2,1)S(1)} %bitcast_dynamic-update-slice_fusion, s32[]{:T(128)} %bitcast.170), kind=kOutput, calls=%fused_computation.60 | convolution fusion | flops 2147483648 | bytes 19398660 | tf_op jit(solution)/shard_map/ldis,djs->lij/dot_general | solution.py:49
  403.0 8.2 %fusion.89 = f32[1,129,32,128]{3,2,1,0:T(8,128)S(1)} fusion(f32[1,129,32,128]{3,2,1,0:T(8,128)S(1)} %fusion.83, bf16[32,8,32,1024]{3,2,1,0:T(8,128)(2,1)} %copy-done.1, bf16[5,8,128,1024]{3,2,1,0:T(8,128)(2,1)S(1)} %bitcast_dynamic-update-slice_fusion, s32[]{:T(128)} %bitcast.170), kind=kOutput, calls=%fused_computation.62 | convolution fusion | flops 2147483648 | bytes 19398660 | tf_op jit(solution)/shard_map/ldis,djs->lij/dot_general | solution.py:49
  411.2 8.4 %fusion.95 = f32[1,129,32,128]{3,2,1,0:T(8,128)S(1)} fusion(f32[1,129,32,128]{3,2,1,0:T(8,128)S(1)} %fusion.89, bf16[32,8,32,1024]{3,2,1,0:T(8,128)(2,1)} %copy-done.2, bf16[5,8,128,1024]{3,2,1,0:T(8,128)(2,1)S(1)} %bitcast_dynamic-update-slice_fusion, s32[]{:T(128)} %bitcast.170), kind=kOutput, calls=%fused_computation.64 | convolution fusion | flops 2147483648 | bytes 19398660 | tf_op jit(solution)/shard_map/ldis,djs->lij/dot_general | solution.py:49
  419.6 8.2 %fusion.101 = f32[1,129,32,128]{3,2,1,0:T(8,128)S(1)} fusion(f32[1,129,32,128]{3,2,1,0:T(8,128)S(1)} %fusion.95, bf16[32,8,32,1024]{3,2,1,0:T(8,128)(2,1)} %get-tuple-element.7, bf16[5,8,128,1024]{3,2,1,0:T(8,128)(2,1)S(1)} %bitcast_dynamic-update-slice_fusion, s32[]{:T(128)} %bitcast.170), kind=kOutput, calls=%fused_computation.66 | convolution fusion | flops 2147483648 | bytes 19398660 | tf_op jit(solution)/shard_map/ldis,djs->lij/dot_general | solution.py:49
  429.5 3.4 pad_maximum_fusion
  (120 shorter events, 37.7 us)
Async XLA Ops:
  6.5 37.2 %all-gather.2.cloned.1.call-start = ((), (), s32[]{:S(2)}) async-start(), calls=%async_computation | async-start | bytes 2621440 | tf_op jit(solution)/shard_map/all_gather | solution.py:59
  54.2 6.0 %copy-start.3 = (bf16[32,8,32,1024]{3,2,1,0:T(8,128)(2,1)}, bf16[32,8,32,1024]{3,2,1,0:T(8,128)(2,1)S(1)}, u32[]{:S(2)}) copy-start(bf16[32,8,32,1024]{3,2,1,0:T(8,128)(2,1)S(1)} %get-tuple-element.11) | copy-start | bytes 50331652
  70.3 5.7 %copy-start.2 = (bf16[32,8,32,1024]{3,2,1,0:T(8,128)(2,1)}, bf16[32,8,32,1024]{3,2,1,0:T(8,128)(2,1)S(1)}, u32[]{:S(2)}) copy-start(bf16[32,8,32,1024]{3,2,1,0:T(8,128)(2,1)S(1)} %get-tuple-element.15) | copy-start | bytes 50331652
  76.2 18.8 %copy-start = (bf16[8,128,1024]{2,1,0:T(8,128)(2,1)S(1)}, bf16[8,128,1024]{2,1,0:T(8,128)(2,1)}, u32[]{:S(2)}) copy-start(bf16[8,128,1024]{2,1,0:T(8,128)(2,1)} %all-gather.2.cloned.1.call-done) | copy-start | bytes 6291460
  82.1 12.0 %copy-start.1 = (bf16[32,8,32,1024]{3,2,1,0:T(8,128)(2,1)}, bf16[32,8,32,1024]{3,2,1,0:T(8,128)(2,1)S(1)}, u32[]{:S(2)}) copy-start(bf16[32,8,32,1024]{3,2,1,0:T(8,128)(2,1)S(1)} %get-tuple-element.18) | copy-start | bytes 50331652
  95.1 44.9 %collective-permute-start = (bf16[8,128,1024]{2,1,0:T(8,128)(2,1)S(1)}, bf16[8,128,1024]{2,1,0:T(8,128)(2,1)S(1)}, u32[]{:S(2)}, u32[]{:S(2)}) collective-permute-start(bf16[8,128,1024]{2,1,0:T(8,128)(2,1)S(1)} %copy-done), channel_id=1, source_target_pairs={{1,0},{2,1},{3,2},{4,3},{5,4},{6,5},{7,6},{8,7},{9,8},{10,9},{11,1... | collective-permute-start | bytes 6291464 | tf_op jit(solution)/shard_map/ppermute | solution.py:19
  98.0 88.7 %collective-permute-start.1 = (bf16[8,128,1024]{2,1,0:T(8,128)(2,1)S(1)}, bf16[8,128,1024]{2,1,0:T(8,128)(2,1)S(1)}, u32[]{:S(2)}, u32[]{:S(2)}) collective-permute-start(bf16[8,128,1024]{2,1,0:T(8,128)(2,1)S(1)} %copy-done), channel_id=1, source_target_pairs={{2,0},{3,1},{4,2},{5,3},{6,4},{7,5},{8,6},{9,7},{10,8},{11,9},{12,... | collective-permute-start | bytes 6291464 | tf_op jit(solution)/shard_map/ppermute | solution.py:19
  103.5 89.4 %collective-permute-start.2 = (bf16[8,128,1024]{2,1,0:T(8,128)(2,1)S(1)}, bf16[8,128,1024]{2,1,0:T(8,128)(2,1)S(1)}, u32[]{:S(2)}, u32[]{:S(2)}) collective-permute-start(bf16[8,128,1024]{2,1,0:T(8,128)(2,1)S(1)} %copy-done), channel_id=1, source_target_pairs={{3,0},{4,1},{5,2},{6,3},{7,4},{8,5},{9,6},{10,7},{11,8},{12,9},{13... | collective-permute-start | bytes 6291464 | tf_op jit(solution)/shard_map/ppermute | solution.py:19
  105.5 221.4 %collective-permute-start.3 = (bf16[8,128,1024]{2,1,0:T(8,128)(2,1)S(1)}, bf16[8,128,1024]{2,1,0:T(8,128)(2,1)S(1)}, u32[]{:S(2)}, u32[]{:S(2)}) collective-permute-start(bf16[8,128,1024]{2,1,0:T(8,128)(2,1)S(1)} %copy-done), channel_id=1, source_target_pairs={{4,0},{5,1},{6,2},{7,3},{8,4},{9,5},{10,6},{11,7},{12,8},{13,9},{1... | collective-permute-start | bytes 6291464 | tf_op jit(solution)/shard_map/ppermute | solution.py:19
Sparse Core Ops, SparseCore 0:
  11.3 32.4 all-gather.1
where the time goes:
time: 449 us; the launch traced here: 440 us
  waiting for transfers between devices  235 us (52%)
  matrix products  101 us (22%)
  local copies, waits for them, and re-layouts  68.6 us (15%)
  between operations  18.3 us (4%)
  other arithmetic  8.86 us (2%)
  starting transfers between devices  8.11 us (2%)
    ppermute x4, waiting for transfers between devices, passed_along(): return lax.ppermute(array, axis, pairs)  207 us
    dot_general x15, matrix products, correlate(): jnp.einsum('ldis,djs->lij', shifted, partner, preferred_element_type=jnp....  101 us
    unnamed x128, local copies, waits for them, and re-layouts  61.7 us
    all_gather x1, waiting for transfers between devices, local(): local_days = lax.all_gather(whitened, 'day', axis=0, tiled=True)  27.8 us
  transfers between devices with their start and end apart: 5, of which 5 were waited for; matrix products, arithmetic and copies ran while one was open for 4% of the time, Pallas kernels for 0%

commit v1 on v0

v1 whole, which is shorter than its diff:
```python
import functools
import jax
import jax.numpy as jnp
from jax import lax
from jax.experimental import pallas as pl
from jax.experimental.pallas import tpu as pltpu
from jax.sharding import PartitionSpec as P

BW = 128
SAMPLES = 1024
MAXLAG = 64
REACH = 4
TILES_DEV = 3
LAGS = 2 * MAXLAG + 1
SHIFTS = MAXLAG + 1
GROUP = 13
GROUPS = SHIFTS // GROUP
BF = jnp.bfloat16


def whiten_kernel(raw_ref, out_ref):
    values = raw_ref[...].astype(jnp.float32)
    centred = values - jnp.mean(values, axis=-1, keepdims=True)
    spread = jnp.mean(centred * centred, axis=-1, keepdims=True)
    out_ref[...] = (centred * lax.rsqrt(spread + 1e-06)).astype(BF)


def whiten(strain_raw):
    days, chans, samples = strain_raw.shape
    spec = pl.BlockSpec((days, 32, samples), lambda i: (0, i, 0))
    return pl.pallas_call(
        whiten_kernel,
        grid=(chans // 32,),
        in_specs=[spec],
        out_specs=spec,
        out_shape=jax.ShapeDtypeStruct(strain_raw.shape, BF),
        cost_estimate=pl.CostEstimate(
            flops=8 * strain_raw.size, bytes_accessed=4 * strain_raw.size, transcendentals=0
        ),
        name="whiten",
    )(strain_raw)


def correlate_kernel(sets, reach, first, norm, win, *refs):
    per_set = 1 + len(reach)
    blocks = [refs[s * per_set : (s + 1) * per_set] for s in range(sets)]
    refs = refs[sets * per_set :]
    if not first:
        refs = refs[1:]
    out_ref, araw, braw, left, right, acc, *rest = refs
    shifted, (sem_a, sem_b, sem_in, sem_out) = rest[:GROUPS], rest[GROUPS:]
    days = araw.shape[1]
    rows = araw.shape[2]
    row0 = pl.multiple_of(win[0] * rows, rows)

    def live(k):
        dist = win[1 + k]
        if first and len(reach) == REACH + 1:
            return dist >= 0
        hit = dist == reach[0]
        for e in reach[1:]:
            hit = jnp.logical_or(hit, dist == e)
        return hit

    lives = [live(k) for k in range(TILES_DEV)]
    any_live = jnp.logical_or(jnp.logical_or(lives[0], lives[1]), lives[2])

    def copy_in(k):
        return pltpu.make_async_copy(out_ref.at[k], acc.at[k], sem_in.at[k])

    def copy_out(k):
        return pltpu.make_async_copy(acc.at[k], out_ref.at[k], sem_out.at[k])

    def copy_left(s):
        return pltpu.make_async_copy(
            blocks[s][0].at[:, pl.ds(row0, rows), :], araw.at[s], sem_a.at[s]
        )

    @pl.when(any_live)
    def _():
        for s in range(sets):
            copy_left(s).start()
            for k in range(TILES_DEV):
                for n, e in enumerate(reach):

                    @pl.when(win[1 + k] == e)
                    def _():
                        pltpu.make_async_copy(
                            blocks[s][1 + n], braw.at[s, k], sem_b.at[s, k]
                        ).start()

        if not first:
            for k in range(TILES_DEV):

                @pl.when(lives[k])
                def _():
                    copy_in(k).start()

        if not first:
            for k in range(TILES_DEV):

                @pl.when(lives[k])
                def _():
                    copy_in(k).wait()

        gap = jnp.zeros((rows, MAXLAG), BF)
        gap_b = jnp.zeros((BW, MAXLAG), BF)

        def make_shift(g):
            for i in range(GROUP):
                shift = g * GROUP + i
                value = left[...]
                if shift:
                    value = pltpu.roll(value, shift, 1)
                shifted[g][i * rows : (i + 1) * rows, :] = value

        def one_set(s, carry):
            pltpu.make_async_copy(
                blocks[0][0].at[:, pl.ds(0, rows), :], araw.at[s], sem_a.at[s]
            ).wait()
            left[...] = jnp.concatenate(
                [p for d in range(days) for p in (araw[s, d], gap)], 1
            )

            def one_slot(k, seen):
                dist = win[1 + k]
                hit = dist == reach[0]
                for e in reach[1:]:
                    hit = jnp.logical_or(hit, dist == e)

                def work(with_shift):
                    pltpu.make_async_copy(
                        blocks[0][1], braw.at[s, k], sem_b.at[s, k]
                    ).wait()
                    right[0:BW, :] = jnp.concatenate(
                        [p for d in range(days) for p in (gap_b, braw[s, k, d])], 1
                    )
                    right[BW : 2 * BW, :] = jnp.concatenate(
                        [p for d in range(days) for p in (braw[s, k, d], gap_b)], 1
                    )
                    if with_shift:
                        make_shift(0)
                    for g in range(GROUPS):
                        if with_shift and g + 1 < GROUPS:
                            make_shift(g + 1)
                        part = lax.dot_general(
                            shifted[g][...],
                            right[...],
                            (((1,), (1,)), ((), ())),
                            preferred_element_type=jnp.float32,
                        )
                        part = part * norm
                        low = part[:, :BW].reshape(GROUP, rows, BW)
                        high = part[:, BW:].reshape(GROUP, rows, BW)
                        lo_at = pl.ds(g * GROUP, GROUP)
                        hi_at = pl.ds(MAXLAG + g * GROUP, GROUP)
                        if g == GROUPS - 1:
                            lo_at = pl.ds(g * GROUP, GROUP - 1)
                            low = low[: GROUP - 1]
                        if sets == 1 and first:
                            acc[k, lo_at] = low
                            acc[k, hi_at] = high
                        else:
                            acc[k, lo_at] += low
                            acc[k, hi_at] += high

                @pl.when(jnp.logical_and(hit, seen == 0))
                def _():
                    work(True)

                @pl.when(jnp.logical_and(hit, seen != 0))
                def _():
                    work(False)

                @pl.when(jnp.logical_and(hit, s == sets - 1))
                def _():
                    copy_out(k).start()

                return seen + hit.astype(jnp.int32)

            lax.fori_loop(0, TILES_DEV, one_slot, jnp.int32(0))
            return carry

        lax.fori_loop(0, sets, one_set, 0)

    if first:
        for k in range(TILES_DEV):

            @pl.when(jnp.logical_not(lives[k]))
            def _():
                acc[k] = jnp.zeros(acc.shape[1:], jnp.float32)
                copy_out(k).start()

        for k in range(TILES_DEV):
            copy_out(k).wait()
    else:
        for k in range(TILES_DEV):

            @pl.when(lives[k])
            def _():
                copy_out(k).wait()


def correlate(sets, reach, scalars, total, rows, norm, name):
    days = sets[0][0].shape[0]
    count = len(sets)
    span = days * (SAMPLES + MAXLAG)
    operands = []
    for own, partners in sets:
        operands += [own] + [partners[e] for e in reach]
    first = total is None
    aliases = {}
    if not first:
        aliases = {1 + len(operands): 0}
        operands.append(total)
    tile = (TILES_DEV, LAGS, rows, BW)
    any_spec = pl.BlockSpec(memory_space=pl.ANY)
    flops = 2 * 2 * count * TILES_DEV * SHIFTS * rows * BW * span * 2 // 2
    return pl.pallas_call(
        functools.partial(correlate_kernel, count, reach, first, norm),
        grid_spec=pltpu.PrefetchScalarGridSpec(
            num_scalar_prefetch=1,
            grid=(1,),
            in_specs=[any_spec] * len(operands),
            out_specs=any_spec,
            scratch_shapes=[
                pltpu.VMEM((count, days, rows, SAMPLES), BF),
                pltpu.VMEM((count, TILES_DEV, days, BW, SAMPLES), BF),
                pltpu.VMEM((rows, span), BF),
                pltpu.VMEM((2 * BW, span), BF),
                pltpu.VMEM(tile, jnp.float32),
            ]
            + [pltpu.VMEM((GROUP * rows, span), BF)] * GROUPS
            + [
                pltpu.SemaphoreType.DMA((count,)),
                pltpu.SemaphoreType.DMA((count, TILES_DEV)),
                pltpu.SemaphoreType.DMA((TILES_DEV,)),
                pltpu.SemaphoreType.DMA((TILES_DEV,)),
            ],
        ),
        out_shape=jax.ShapeDtypeStruct(tile, jnp.float32),
        input_output_aliases=aliases,
        compiler_params=pltpu.CompilerParams(vmem_limit_bytes=40 << 20),
        cost_estimate=pl.CostEstimate(
            flops=flops, bytes_accessed=8 << 20, transcendentals=0
        ),
        name=name,
    )(scalars, *operands)


def moved(array, axis, by):
    devices = lax.axis_size(axis)
    if axis == "day":
        pairs = [(i, (i + by) % devices) for i in range(devices)]
    else:
        pairs = [(i, i + by) for i in range(devices) if 0 <= i + by < devices]
    return lax.ppermute(array, axis, pairs)


def swapped(array):
    devices = lax.axis_size("chan")
    return lax.ppermute(array, "chan", [(i, i ^ 1) for i in range(devices)])


def local(strain_raw, pair_dist):
    day = lax.axis_index("day")
    even = lax.axis_index("chan") % 2 == 0
    rows = BW // lax.axis_size("day")
    total_days = strain_raw.shape[0] * lax.axis_size("day")
    norm = float((SAMPLES * total_days) ** -0.5)
    scalars = jnp.concatenate([day.astype(jnp.int32)[None], pair_dist[0].astype(jnp.int32)])

    own = whiten(strain_raw)
    z2 = moved(own, "chan", -2)
    own_p, own_m = moved(own, "day", 1), moved(own, "day", -1)
    z4 = moved(own, "chan", -4)
    own_2 = moved(own, "day", 2)
    z2_p, z2_m = moved(z2, "day", 1), moved(z2, "day", -1)
    z2_2, z4_2 = moved(own_2, "chan", -2), moved(own_2, "chan", -4)
    z4_p, z4_m = moved(z4, "day", 1), moved(z4, "day", -1)

    def with_pair(mine, two, four):
        odd_ones = swapped(jnp.where(even, two, mine))
        even_ones = swapped(jnp.where(even, four, two))
        return mine, {0: mine, 1: odd_ones, 2: two, 3: even_ones, 4: four}

    reach = tuple(range(REACH + 1))
    tiles = correlate([with_pair(own, z2, z4)], reach, scalars, None, rows, norm, "near_days")
    others = [
        with_pair(own_p, z2_p, z4_p),
        with_pair(own_m, z2_m, z4_m),
        with_pair(own_2, z2_2, z4_2),
    ]
    return correlate(others, reach, scalars, tiles, rows, norm, "far_days")


def solution(mesh):
    placed = (P("day", "chan", None), P("chan", None))
    return jax.shard_map(
        local, mesh=mesh, in_specs=placed, out_specs=P("chan", None, "day", None), check_vma=False
    )
```

time: 449 us -> 123 us (0.27)
  the two profiles are of different devices: /device:TPU:64 before, /device:TPU:56 now
where the time goes in v1:
time: 123 us; the launch traced here: 122 us
  Pallas kernels  46.3 us (38%)
  waiting for transfers between devices  45.6 us (37%)
  starting transfers between devices  27.4 us (22%)
  other arithmetic  2.16 us (2%)
    ppermute x11, waiting for transfers between devices, moved(): return lax.ppermute(array, axis, pairs)  45.5 us
    pallas_call x2, Pallas kernels, correlate(): pl.pallas_call(functools.partial(correlate_kernel, count, reach, first, n...  42.7 us
    ppermute x11, starting transfers between devices, moved(): return lax.ppermute(array, axis, pairs)  24.1 us
    pallas_call x1, Pallas kernels, whiten(): pl.pallas_call(whiten_kernel, grid=(chans // 32,), in_specs=[spec], out_s...  3.55 us
    ppermute x8, starting transfers between devices, swapped(): return lax.ppermute(array, 'chan', [(i, i ^ 1) for i in range(devices)])  3.3 us
  transfers between devices with their start and end apart: 19, of which 7 were waited for; matrix products, arithmetic and copies ran while one was open for 2% of the time, Pallas kernels for 9%

profile of v1, /device:TPU:56, one launch (start us, length us, event | category | flops | bytes accessed | tf_op | source)
XLA Modules:
  0.0 121.7 jit_solution(14964784937734062187)
XLA Ops:
  0.0 3.5 %whiten.1.refs_0_.refs_1_ = bf16[2,128,1024]{2,1,0:T(8,128)(2,1)} custom-call(bf16[2,128,1024]{2,1,0:T(8,128)(2,1)} %raw_ref.1), custom_call_target="tpu_custom_call" | custom-call | flops 2097152 | bytes 1048576 | tf_op jit(solution)/shard_map/whiten/pallas_call | solution.py:31
  3.6 0.0 copy-start
  3.6 5.2 %collective-permute-start.4 = (bf16[2,128,1024]{2,1,0:T(8,128)(2,1)}, bf16[2,128,1024]{2,1,0:T(8,128)(2,1)S(1)}, u32[]{:S(2)}, u32[]{:S(2)}) collective-permute-start(bf16[2,128,1024]{2,1,0:T(8,128)(2,1)} %whiten.1.refs_0_.refs_1_), channel_id=1, source_target_pairs={{4,0},{5,1},{6,2},{7,3},{8,4},{9,5},{10,6},{11,7},{12,8},{13,9},{1... | collective-permute-start | bytes 1572872 | tf_op jit(solution)/shard_map/ppermute | solution.py:257
  8.7 2.9 %collective-permute-start.1 = (bf16[2,128,1024]{2,1,0:T(8,128)(2,1)}, bf16[2,128,1024]{2,1,0:T(8,128)(2,1)}, u32[]{:S(2)}, u32[]{:S(2)}) collective-permute-start(bf16[2,128,1024]{2,1,0:T(8,128)(2,1)} %whiten.1.refs_0_.refs_1_), channel_id=1, source_target_pairs={{2,0},{3,1},{4,2},{5,3},{6,4},{7,5},{8,6},{9,7},{10,8},{11,9},{12,... | collective-permute-start | bytes 1572872 | tf_op jit(solution)/shard_map/ppermute | solution.py:257
  11.7 3.1 %collective-permute-start.12 = (bf16[2,128,1024]{2,1,0:T(8,128)(2,1)}, bf16[2,128,1024]{2,1,0:T(8,128)(2,1)S(1)}, u32[]{:S(2)}, u32[]{:S(2)}) collective-permute-start(bf16[2,128,1024]{2,1,0:T(8,128)(2,1)} %whiten.1.refs_0_.refs_1_), channel_id=1, source_target_pairs={{0,64},{32,96},{64,0},{96,32},{1,65},{33,97},{65,1},{97,33},{2,66}... | collective-permute-start | bytes 1572872 | tf_op jit(solution)/shard_map/ppermute | solution.py:257
  14.8 0.6 collective-permute-start
  15.4 6.8 %collective-permute-done.4.refs_5_ = bf16[2,128,1024]{2,1,0:T(8,128)(2,1)S(1)} collective-permute-done((bf16[2,128,1024]{2,1,0:T(8,128)(2,1)}, bf16[2,128,1024]{2,1,0:T(8,128)(2,1)S(1)}, u32[]{:S(2)}, u32[]{:S(2)}) %collective-permute-start.4) | collective-permute-done | bytes 524320 | tf_op jit(solution)/shard_map/ppermute | solution.py:257
  22.1 1.5 %collective-permute-start.5 = (bf16[2,128,1024]{2,1,0:T(8,128)(2,1)S(1)}, bf16[2,128,1024]{2,1,0:T(8,128)(2,1)S(1)}, u32[]{:S(2)}, u32[]{:S(2)}) collective-permute-start(bf16[2,128,1024]{2,1,0:T(8,128)(2,1)S(1)} %collective-permute-done.4.refs_5_), channel_id=1, source_target_pairs={{0,32},{32,64},{64,96},{96,0},{1,33},{33,65},{65,97},{97,1},{2,34}... | collective-permute-start | bytes 1572872 | tf_op jit(solution)/shard_map/ppermute | solution.py:257
  23.6 8.7 %collective-permute-done.1.refs_3_ = bf16[2,128,1024]{2,1,0:T(8,128)(2,1)} collective-permute-done((bf16[2,128,1024]{2,1,0:T(8,128)(2,1)}, bf16[2,128,1024]{2,1,0:T(8,128)(2,1)}, u32[]{:S(2)}, u32[]{:S(2)}) %collective-permute-start.1) | collective-permute-done | bytes 524320 | tf_op jit(solution)/shard_map/ppermute | solution.py:257
  32.3 1.5 %collective-permute-start.2 = (bf16[2,128,1024]{2,1,0:T(8,128)(2,1)}, bf16[2,128,1024]{2,1,0:T(8,128)(2,1)S(1)}, u32[]{:S(2)}, u32[]{:S(2)}) collective-permute-start(bf16[2,128,1024]{2,1,0:T(8,128)(2,1)} %collective-permute-done.1.refs_3_), channel_id=1, source_target_pairs={{0,32},{32,64},{64,96},{96,0},{1,33},{33,65},{65,97},{97,1},{2,34}... | collective-permute-start | bytes 1572872 | tf_op jit(solution)/shard_map/ppermute | solution.py:257
  33.8 1.7 %collective-permute-start.7 = (bf16[2,128,1024]{2,1,0:T(8,128)(2,1)}, bf16[2,128,1024]{2,1,0:T(8,128)(2,1)}, u32[]{:S(2)}, u32[]{:S(2)}) collective-permute-start(bf16[2,128,1024]{2,1,0:T(8,128)(2,1)} %whiten.1.refs_0_.refs_1_), channel_id=1, source_target_pairs={{0,96},{32,0},{64,32},{96,64},{1,97},{33,1},{65,33},{97,65},{2,98}... | collective-permute-start | bytes 1572872 | tf_op jit(solution)/shard_map/ppermute | solution.py:257
  35.5 0.7 pad_add_fusion.win
  36.3 0.0 collective-permute-done.12.refs_12_.refs_13_
  36.3 1.6 %collective-permute-start.10 = (bf16[2,128,1024]{2,1,0:T(8,128)(2,1)S(1)}, bf16[2,128,1024]{2,1,0:T(8,128)(2,1)S(1)}, u32[]{:S(2)}, u32[]{:S(2)}) collective-permute-start(bf16[2,128,1024]{2,1,0:T(8,128)(2,1)S(1)} %collective-permute-done.4.refs_5_), channel_id=1, source_target_pairs={{0,96},{32,0},{64,32},{96,64},{1,97},{33,1},{65,33},{97,65},{2,98}... | collective-permute-start | bytes 1572872 | tf_op jit(solution)/shard_map/ppermute | solution.py:257
  37.8 0.9 collective-permute-done.refs_0_.refs_1_
  38.7 1.5 %collective-permute-start.8 = (bf16[2,128,1024]{2,1,0:T(8,128)(2,1)}, bf16[2,128,1024]{2,1,0:T(8,128)(2,1)S(1)}, u32[]{:S(2)}, u32[]{:S(2)}) collective-permute-start(bf16[2,128,1024]{2,1,0:T(8,128)(2,1)} %collective-permute-done.1.refs_3_), channel_id=1, source_target_pairs={{0,96},{32,0},{64,32},{96,64},{1,97},{33,1},{65,33},{97,65},{2,98}... | collective-permute-start | bytes 1572872 | tf_op jit(solution)/shard_map/ppermute | solution.py:257
  40.2 1.2 broadcast_select_fusion
  41.3 8.5 %collective-permute-done.5.refs_5_ = bf16[2,128,1024]{2,1,0:T(8,128)(2,1)S(1)} collective-permute-done((bf16[2,128,1024]{2,1,0:T(8,128)(2,1)S(1)}, bf16[2,128,1024]{2,1,0:T(8,128)(2,1)S(1)}, u32[]{:S(2)}, u32[]{:S(2)}) %collective-permute-start.5) | collective-permute-done | bytes 524320 | tf_op jit(solution)/shard_map/ppermute | solution.py:257
  49.8 1.9 %collective-permute-start.15 = (bf16[2,128,1024]{2,1,0:T(8,128)(2,1)S(1)}, bf16[2,128,1024]{2,1,0:T(8,128)(2,1)S(1)}, u32[]{:S(2)}, u32[]{:S(2)}) collective-permute-start(bf16[2,128,1024]{2,1,0:T(8,128)(2,1)S(1)} %collective-permute-done.12.refs_12_.refs_13_), channel_id=1, source_target_pairs={{4,0},{5,1},{6,2},{7,3},{8,4},{9,5},{10,6},{11,7},{12,8},{13,9},{1... | collective-permute-start | bytes 1572872 | tf_op jit(solution)/shard_map/ppermute | solution.py:257
  51.8 8.5 %collective-permute-done.2.refs_3_ = bf16[2,128,1024]{2,1,0:T(8,128)(2,1)S(1)} collective-permute-done((bf16[2,128,1024]{2,1,0:T(8,128)(2,1)}, bf16[2,128,1024]{2,1,0:T(8,128)(2,1)S(1)}, u32[]{:S(2)}, u32[]{:S(2)}) %collective-permute-start.2) | collective-permute-done | bytes 524320 | tf_op jit(solution)/shard_map/ppermute | solution.py:257
  60.3 2.6 %collective-permute-start.13 = (bf16[2,128,1024]{2,1,0:T(8,128)(2,1)S(1)}, bf16[2,128,1024]{2,1,0:T(8,128)(2,1)S(1)}, u32[]{:S(2)}, u32[]{:S(2)}) collective-permute-start(bf16[2,128,1024]{2,1,0:T(8,128)(2,1)S(1)} %collective-permute-done.12.refs_12_.refs_13_), channel_id=1, source_target_pairs={{2,0},{3,1},{4,2},{5,3},{6,4},{7,5},{8,6},{9,7},{10,8},{11,9},{12,... | collective-permute-start | bytes 1572872 | tf_op jit(solution)/shard_map/ppermute | solution.py:257
  62.9 0.1 broadcast_select_fusion.6
  63.0 0.0 collective-permute-done.7.refs_6_.refs_7_
  63.0 0.1 collective-permute-start.18
  63.1 0.0 collective-permute-done.10.refs_11_
  63.1 0.5 collective-permute-start.17
  63.6 6.4 %collective-permute-done.8.refs_9_ = bf16[2,128,1024]{2,1,0:T(8,128)(2,1)S(1)} collective-permute-done((bf16[2,128,1024]{2,1,0:T(8,128)(2,1)}, bf16[2,128,1024]{2,1,0:T(8,128)(2,1)S(1)}, u32[]{:S(2)}, u32[]{:S(2)}) %collective-permute-start.8) | collective-permute-done | bytes 524320 | tf_op jit(solution)/shard_map/ppermute | solution.py:257
  70.0 0.0 collective-permute-start.6
  70.0 0.1 broadcast_select_fusion.4
  70.1 0.0 collective-permute-done.15.refs_17_
  70.1 1.6 %collective-permute-start.3 = (bf16[2,128,1024]{2,1,0:T(8,128)(2,1)S(1)}, bf16[2,128,1024]{2,1,0:T(8,128)(2,1)S(1)}, u32[]{:S(2)}, u32[]{:S(2)}) collective-permute-start(bf16[2,128,1024]{2,1,0:T(8,128)(2,1)S(1)} %get-tuple-element.12), channel_id=1, source_target_pairs={{0,1},{1,0},{2,3},{3,2},{4,5},{5,4},{6,7},{7,6},{8,9},{9,8},{10,11... | collective-permute-start | bytes 1572872 | tf_op jit(solution)/shard_map/ppermute | solution.py:262
  71.8 5.8 %collective-permute-done.13.refs_15_ = bf16[2,128,1024]{2,1,0:T(8,128)(2,1)S(1)} collective-permute-done((bf16[2,128,1024]{2,1,0:T(8,128)(2,1)S(1)}, bf16[2,128,1024]{2,1,0:T(8,128)(2,1)S(1)}, u32[]{:S(2)}, u32[]{:S(2)}) %collective-permute-start.13) | collective-permute-done | bytes 524320 | tf_op jit(solution)/shard_map/ppermute | solution.py:257
  77.5 0.0 collective-permute-start.11
  77.5 0.1 broadcast_select_fusion.2
  77.6 0.0 collective-permute-done.18.refs_4_
  77.6 0.6 collective-permute-start.9
  78.2 0.0 collective-permute-done.17.refs_2_
  78.2 0.1 collective-permute-start.16
  78.3 0.0 collective-permute-done.6.refs_4_
  78.3 0.4 collective-permute-start.14
  78.7 0.0 copy-done
  78.7 10.7 %near_days.1.refs_18_ = f32[3,129,32,128]{3,2,1,0:T(8,128)} custom-call(s32[4]{0:T(128)S(1)} %pad_add_fusion.win, bf16[2,128,1024]{2,1,0:T(8,128)(2,1)S(1)} %copy-done, bf16[2,128,1024]{2,1,0:T(8,128)(2,1)S(1)} %copy-done, bf16[2,128,1024]{2,1,0:T(8,128)(2,1)S(1)} %collective-permute-done.17.refs_2_, bf16[2,128,1024]{2,1,0:T(8,128)(2,1)} %collective-permute-done.1.refs_3_, ...), custom_call_target="tpu_custom_call" | custom-call | flops 6952058880 | bytes 8388608 | tf_op jit(solution)/shard_map/near_days/pallas_call | solution.py:219
  89.5 0.0 collective-permute-done.3.refs_2_
  89.5 0.0 collective-permute-done.11.refs_10_
  89.5 0.0 collective-permute-done.9.refs_8_
  89.5 0.0 collective-permute-done.16.refs_16_
  89.5 0.0 collective-permute-done.14.refs_14_
  89.5 32.0 %far_days.1 = f32[3,129,32,128]{3,2,1,0:T(8,128)} custom-call(s32[4]{0:T(128)S(1)} %pad_add_fusion.win, bf16[2,128,1024]{2,1,0:T(8,128)(2,1)S(1)} %collective-permute-done.refs_0_.refs_1_, bf16[2,128,1024]{2,1,0:T(8,128)(2,1)S(1)} %collective-permute-done.refs_0_.refs_1_, ...), custom_call_target="tpu_custom_call", output_to_operand_aliasing={{}: (19, {})} | custom-call | flops 20856176640 | bytes 8388608 | tf_op jit(solution)/shard_map/far_days/pallas_call | solution.py:219
Async XLA Ops:
  3.6 75.2 %copy-start = (bf16[2,128,1024]{2,1,0:T(8,128)(2,1)S(1)}, bf16[2,128,1024]{2,1,0:T(8,128)(2,1)}, u32[]{:S(2)}) copy-start(bf16[2,128,1024]{2,1,0:T(8,128)(2,1)} %whiten.1.refs_0_.refs_1_) | copy-start | bytes 1572868
  3.6 18.6 %collective-permute-start.4 = (bf16[2,128,1024]{2,1,0:T(8,128)(2,1)}, bf16[2,128,1024]{2,1,0:T(8,128)(2,1)S(1)}, u32[]{:S(2)}, u32[]{:S(2)}) collective-permute-start(bf16[2,128,1024]{2,1,0:T(8,128)(2,1)} %whiten.1.refs_0_.refs_1_), channel_id=1, source_target_pairs={{4,0},{5,1},{6,2},{7,3},{8,4},{9,5},{10,6},{11,7},{12,8},{13,9},{1... | collective-permute-start | bytes 1572872 | tf_op jit(solution)/shard_map/ppermute | solution.py:257
  8.7 23.5 %collective-permute-start.1 = (bf16[2,128,1024]{2,1,0:T(8,128)(2,1)}, bf16[2,128,1024]{2,1,0:T(8,128)(2,1)}, u32[]{:S(2)}, u32[]{:S(2)}) collective-permute-start(bf16[2,128,1024]{2,1,0:T(8,128)(2,1)} %whiten.1.refs_0_.refs_1_), channel_id=1, source_target_pairs={{2,0},{3,1},{4,2},{5,3},{6,4},{7,5},{8,6},{9,7},{10,8},{11,9},{12,... | collective-permute-start | bytes 1572872 | tf_op jit(solution)/shard_map/ppermute | solution.py:257
  11.7 24.6 %collective-permute-start.12 = (bf16[2,128,1024]{2,1,0:T(8,128)(2,1)}, bf16[2,128,1024]{2,1,0:T(8,128)(2,1)S(1)}, u32[]{:S(2)}, u32[]{:S(2)}) collective-permute-start(bf16[2,128,1024]{2,1,0:T(8,128)(2,1)} %whiten.1.refs_0_.refs_1_), channel_id=1, source_target_pairs={{0,64},{32,96},{64,0},{96,32},{1,65},{33,97},{65,1},{97,33},{2,66}... | collective-permute-start | bytes 1572872 | tf_op jit(solution)/shard_map/ppermute | solution.py:257
  14.8 23.9 %collective-permute-start = (bf16[2,128,1024]{2,1,0:T(8,128)(2,1)}, bf16[2,128,1024]{2,1,0:T(8,128)(2,1)S(1)}, u32[]{:S(2)}, u32[]{:S(2)}) collective-permute-start(bf16[2,128,1024]{2,1,0:T(8,128)(2,1)} %whiten.1.refs_0_.refs_1_), channel_id=1, source_target_pairs={{0,32},{32,64},{64,96},{96,0},{1,33},{33,65},{65,97},{97,1},{2,34}... | collective-permute-start | bytes 1572872 | tf_op jit(solution)/shard_map/ppermute | solution.py:257
  22.1 27.7 %collective-permute-start.5 = (bf16[2,128,1024]{2,1,0:T(8,128)(2,1)S(1)}, bf16[2,128,1024]{2,1,0:T(8,128)(2,1)S(1)}, u32[]{:S(2)}, u32[]{:S(2)}) collective-permute-start(bf16[2,128,1024]{2,1,0:T(8,128)(2,1)S(1)} %collective-permute-done.4.refs_5_), channel_id=1, source_target_pairs={{0,32},{32,64},{64,96},{96,0},{1,33},{33,65},{65,97},{97,1},{2,34}... | collective-permute-start | bytes 1572872 | tf_op jit(solution)/shard_map/ppermute | solution.py:257
  32.3 28.0 %collective-permute-start.2 = (bf16[2,128,1024]{2,1,0:T(8,128)(2,1)}, bf16[2,128,1024]{2,1,0:T(8,128)(2,1)S(1)}, u32[]{:S(2)}, u32[]{:S(2)}) collective-permute-start(bf16[2,128,1024]{2,1,0:T(8,128)(2,1)} %collective-permute-done.1.refs_3_), channel_id=1, source_target_pairs={{0,32},{32,64},{64,96},{96,0},{1,33},{33,65},{65,97},{97,1},{2,34}... | collective-permute-start | bytes 1572872 | tf_op jit(solution)/shard_map/ppermute | solution.py:257
  33.8 29.2 %collective-permute-start.7 = (bf16[2,128,1024]{2,1,0:T(8,128)(2,1)}, bf16[2,128,1024]{2,1,0:T(8,128)(2,1)}, u32[]{:S(2)}, u32[]{:S(2)}) collective-permute-start(bf16[2,128,1024]{2,1,0:T(8,128)(2,1)} %whiten.1.refs_0_.refs_1_), channel_id=1, source_target_pairs={{0,96},{32,0},{64,32},{96,64},{1,97},{33,1},{65,33},{97,65},{2,98}... | collective-permute-start | bytes 1572872 | tf_op jit(solution)/shard_map/ppermute | solution.py:257
  36.3 26.8 %collective-permute-start.10 = (bf16[2,128,1024]{2,1,0:T(8,128)(2,1)S(1)}, bf16[2,128,1024]{2,1,0:T(8,128)(2,1)S(1)}, u32[]{:S(2)}, u32[]{:S(2)}) collective-permute-start(bf16[2,128,1024]{2,1,0:T(8,128)(2,1)S(1)} %collective-permute-done.4.refs_5_), channel_id=1, source_target_pairs={{0,96},{32,0},{64,32},{96,64},{1,97},{33,1},{65,33},{97,65},{2,98}... | collective-permute-start | bytes 1572872 | tf_op jit(solution)/shard_map/ppermute | solution.py:257
  38.7 31.3 %collective-permute-start.8 = (bf16[2,128,1024]{2,1,0:T(8,128)(2,1)}, bf16[2,128,1024]{2,1,0:T(8,128)(2,1)S(1)}, u32[]{:S(2)}, u32[]{:S(2)}) collective-permute-start(bf16[2,128,1024]{2,1,0:T(8,128)(2,1)} %collective-permute-done.1.refs_3_), channel_id=1, source_target_pairs={{0,96},{32,0},{64,32},{96,64},{1,97},{33,1},{65,33},{97,65},{2,98}... | collective-permute-start | bytes 1572872 | tf_op jit(solution)/shard_map/ppermute | solution.py:257
  49.8 20.3 %collective-permute-start.15 = (bf16[2,128,1024]{2,1,0:T(8,128)(2,1)S(1)}, bf16[2,128,1024]{2,1,0:T(8,128)(2,1)S(1)}, u32[]{:S(2)}, u32[]{:S(2)}) collective-permute-start(bf16[2,128,1024]{2,1,0:T(8,128)(2,1)S(1)} %collective-permute-done.12.refs_12_.refs_13_), channel_id=1, source_target_pairs={{4,0},{5,1},{6,2},{7,3},{8,4},{9,5},{10,6},{11,7},{12,8},{13,9},{1... | collective-permute-start | bytes 1572872 | tf_op jit(solution)/shard_map/ppermute | solution.py:257
  60.3 17.2 %collective-permute-start.13 = (bf16[2,128,1024]{2,1,0:T(8,128)(2,1)S(1)}, bf16[2,128,1024]{2,1,0:T(8,128)(2,1)S(1)}, u32[]{:S(2)}, u32[]{:S(2)}) collective-permute-start(bf16[2,128,1024]{2,1,0:T(8,128)(2,1)S(1)} %collective-permute-done.12.refs_12_.refs_13_), channel_id=1, source_target_pairs={{2,0},{3,1},{4,2},{5,3},{6,4},{7,5},{8,6},{9,7},{10,8},{11,9},{12,... | collective-permute-start | bytes 1572872 | tf_op jit(solution)/shard_map/ppermute | solution.py:257
  63.0 14.6 %collective-permute-start.18 = (bf16[2,128,1024]{2,1,0:T(8,128)(2,1)S(1)}, bf16[2,128,1024]{2,1,0:T(8,128)(2,1)S(1)}, u32[]{:S(2)}, u32[]{:S(2)}) collective-permute-start(bf16[2,128,1024]{2,1,0:T(8,128)(2,1)S(1)} %get-tuple-element.5), channel_id=1, source_target_pairs={{0,1},{1,0},{2,3},{3,2},{4,5},{5,4},{6,7},{7,6},{8,9},{9,8},{10,11... | collective-permute-start | bytes 1572872 | tf_op jit(solution)/shard_map/ppermute | solution.py:262
  63.1 15.1 %collective-permute-start.17 = (bf16[2,128,1024]{2,1,0:T(8,128)(2,1)S(1)}, bf16[2,128,1024]{2,1,0:T(8,128)(2,1)S(1)}, u32[]{:S(2)}, u32[]{:S(2)}) collective-permute-start(bf16[2,128,1024]{2,1,0:T(8,128)(2,1)S(1)} %get-tuple-element.6), channel_id=1, source_target_pairs={{0,1},{1,0},{2,3},{3,2},{4,5},{5,4},{6,7},{7,6},{8,9},{9,8},{10,11... | collective-permute-start | bytes 1572872 | tf_op jit(solution)/shard_map/ppermute | solution.py:262
  70.0 8.3 %collective-permute-start.6 = (bf16[2,128,1024]{2,1,0:T(8,128)(2,1)S(1)}, bf16[2,128,1024]{2,1,0:T(8,128)(2,1)S(1)}, u32[]{:S(2)}, u32[]{:S(2)}) collective-permute-start(bf16[2,128,1024]{2,1,0:T(8,128)(2,1)S(1)} %get-tuple-element.11), channel_id=1, source_target_pairs={{0,1},{1,0},{2,3},{3,2},{4,5},{5,4},{6,7},{7,6},{8,9},{9,8},{10,11... | collective-permute-start | bytes 1572872 | tf_op jit(solution)/shard_map/ppermute | solution.py:262
  70.1 19.3 %collective-permute-start.3 = (bf16[2,128,1024]{2,1,0:T(8,128)(2,1)S(1)}, bf16[2,128,1024]{2,1,0:T(8,128)(2,1)S(1)}, u32[]{:S(2)}, u32[]{:S(2)}) collective-permute-start(bf16[2,128,1024]{2,1,0:T(8,128)(2,1)S(1)} %get-tuple-element.12), channel_id=1, source_target_pairs={{0,1},{1,0},{2,3},{3,2},{4,5},{5,4},{6,7},{7,6},{8,9},{9,8},{10,11... | collective-permute-start | bytes 1572872 | tf_op jit(solution)/shard_map/ppermute | solution.py:262
  77.5 12.0 %collective-permute-start.11 = (bf16[2,128,1024]{2,1,0:T(8,128)(2,1)S(1)}, bf16[2,128,1024]{2,1,0:T(8,128)(2,1)S(1)}, u32[]{:S(2)}, u32[]{:S(2)}) collective-permute-start(bf16[2,128,1024]{2,1,0:T(8,128)(2,1)S(1)} %get-tuple-element.9), channel_id=1, source_target_pairs={{0,1},{1,0},{2,3},{3,2},{4,5},{5,4},{6,7},{7,6},{8,9},{9,8},{10,11... | collective-permute-start | bytes 1572872 | tf_op jit(solution)/shard_map/ppermute | solution.py:262
  77.6 11.9 %collective-permute-start.9 = (bf16[2,128,1024]{2,1,0:T(8,128)(2,1)S(1)}, bf16[2,128,1024]{2,1,0:T(8,128)(2,1)S(1)}, u32[]{:S(2)}, u32[]{:S(2)}) collective-permute-start(bf16[2,128,1024]{2,1,0:T(8,128)(2,1)S(1)} %get-tuple-element.10), channel_id=1, source_target_pairs={{0,1},{1,0},{2,3},{3,2},{4,5},{5,4},{6,7},{7,6},{8,9},{9,8},{10,11... | collective-permute-start | bytes 1572872 | tf_op jit(solution)/shard_map/ppermute | solution.py:262
  78.2 11.3 %collective-permute-start.16 = (bf16[2,128,1024]{2,1,0:T(8,128)(2,1)S(1)}, bf16[2,128,1024]{2,1,0:T(8,128)(2,1)S(1)}, u32[]{:S(2)}, u32[]{:S(2)}) collective-permute-start(bf16[2,128,1024]{2,1,0:T(8,128)(2,1)S(1)} %get-tuple-element.7), channel_id=1, source_target_pairs={{0,1},{1,0},{2,3},{3,2},{4,5},{5,4},{6,7},{7,6},{8,9},{9,8},{10,11... | collective-permute-start | bytes 1572872 | tf_op jit(solution)/shard_map/ppermute | solution.py:262
  78.3 11.2 %collective-permute-start.14 = (bf16[2,128,1024]{2,1,0:T(8,128)(2,1)S(1)}, bf16[2,128,1024]{2,1,0:T(8,128)(2,1)S(1)}, u32[]{:S(2)}, u32[]{:S(2)}) collective-permute-start(bf16[2,128,1024]{2,1,0:T(8,128)(2,1)S(1)} %get-tuple-element.8), channel_id=1, source_target_pairs={{0,1},{1,0},{2,3},{3,2},{4,5},{5,4},{6,7},{7,6},{8,9},{9,8},{10,11... | collective-permute-start | bytes 1572872 | tf_op jit(solution)/shard_map/ppermute | solution.py:262
